TPU v7x, 128 devices: a whole 4x4x4 slice. The times are simulated.
128 devices in a mesh: rep: 8 (over x_lo, z), grp: 16 (over y, x_hi, core).
Axes of the slice: x: 4 (x_hi: 2, x_lo: 2; x = x_hi * 2 + x_lo), y: 4, z: 4, core: 2. Of those that a mesh axis runs over, the one named last changes fastest.
Arguments:
- master_weight: float32 [4096, 14336], P('rep', 'grp'), may hold values from -0.09375 to 0.09375
- first_moment: float32 [4096, 14336], P('rep', 'grp'), may hold values from -6 to 6
- second_moment: float32 [4096, 14336], P('rep', 'grp'), may hold values from 0.25 to 4
- prior_grad: float32 [4096, 14336], P('rep', 'grp'), may hold values from -6 to 6
- tokens: bfloat16 [16384, 4096], P(('rep', 'grp')), may hold values from -6 to 6
- cotangent: bfloat16 [16384, 14336], P(('rep', 'grp')), may hold values from -0.046875 to 0.046875
Outputs:
- new_master: float32 [4096, 14336], P('rep', 'grp')
- first_new: float32 [4096, 14336], P('rep', 'grp')
- second_new: float32 [4096, 14336], P('rep', 'grp')
- grad_sum: float32 [4096, 14336], P('rep', 'grp')
- up_proj: bfloat16 [16384, 14336], P(('rep', 'grp'))
All inputs are finite; a program needn't handle non-finite values.
Results may differ from a plain program's by a relative error of at most 0.015.
Values may be sent and summed in bfloat16 or wider, within the bound.
A program may use at most 128 MiB of HBM per device.

v0:
```python
import jax
import jax.numpy as jnp
from jax import lax
from jax.sharding import PartitionSpec as P

STEP = 100


learning_rate = 0.002
beta_one = 0.9
beta_two = 0.95
epsilon = 1e-08
decay_weight = 0.1
contract_rows = (((0,), (0,)), ((), ()))


def adam_update(master_weight, first_moment, second_moment, prior_grad):
    first_new = beta_one * first_moment + (1.0 - beta_one) * prior_grad
    second_new = beta_two * second_moment + (1.0 - beta_two) * prior_grad * prior_grad
    bias_one = 1.0 - beta_one**STEP
    bias_two = 1.0 - beta_two**STEP
    step_size = first_new / bias_one / (jnp.sqrt(second_new / bias_two) + epsilon)
    new_master = master_weight - learning_rate * (step_size + decay_weight * master_weight)
    return (new_master, first_new, second_new)


def column_term(group_tokens, back_columns):
    return lax.dot_general(
        group_tokens, back_columns, contract_rows, preferred_element_type=jnp.float32
    )


def body(master_weight, first_moment, second_moment, prior_grad, tokens, cotangent):
    new_master, first_new, second_new = adam_update(
        master_weight, first_moment, second_moment, prior_grad
    )
    weight_half = new_master.astype(jnp.bfloat16)
    back_columns = lax.all_to_all(cotangent, "grp", split_axis=1, concat_axis=0, tiled=True)
    weight_columns = lax.all_gather(weight_half, "rep", axis=0, tiled=True)
    group_tokens = lax.all_gather(tokens, "grp", axis=0, tiled=True)
    up_columns = jnp.dot(group_tokens, weight_columns, preferred_element_type=jnp.float32).astype(
        jnp.bfloat16
    )
    grad_sum = lax.psum_scatter(
        column_term(group_tokens, back_columns).astype(jnp.bfloat16),
        "rep",
        scatter_dimension=0,
        tiled=True,
    ).astype(jnp.float32)
    up_proj = lax.all_to_all(up_columns, "grp", split_axis=0, concat_axis=1, tiled=True)
    return (new_master, first_new, second_new, grad_sum, up_proj)


def solution(mesh):
    return jax.shard_map(
        body,
        mesh=mesh,
        in_specs=(
            P("rep", "grp"),
            P("rep", "grp"),
            P("rep", "grp"),
            P("rep", "grp"),
            P(("rep", "grp"), None),
            P(("rep", "grp"), None),
        ),
        out_specs=(
            P("rep", "grp"),
            P("rep", "grp"),
            P("rep", "grp"),
            P("rep", "grp"),
            P(("rep", "grp"), None),
        ),
        check_vma=False,
    )
```

profile of v0, /device:TPU:1, one launch (start us, length us, event | category | flops | bytes accessed | tf_op | source)
XLA Modules:
  0.0 372.7 jit_solution(12011827314552283323)
XLA Ops:
  7.2 0.0 all-gather.3.cloned.1.call-start
  7.2 0.7 all-gather.3.cloned.1.call-update
  7.9 0.0 all-gather.5.cloned.1.call-start
  7.9 6.8 %fusion.1 = (bf16[512,896]{1,0:T(8,128)(2,1)}, f32[512,896]{1,0:T(8,128)}, f32[512,896]{1,0:T(8,128)}, f32[512,896]{1,0:T(8,128)}) fusion(f32[512,896]{1,0:T(8,128)} %param.6, f32[512,896]{1,0:T(8,128)} %param.9, f32[512,896]{1,0:T(8,128)} %param.7, f32[512,896]{1,0:T(8,128)} %param.8), kind=kLoop, calls=%fused_computation.7 | loop fusion | flops 7340032 | bytes 13762560 | tf_op jit(solution)/shard_map/convert_element_type | solution.py:37
  14.7 0.0 all-gather.5.cloned.1.call-update
  14.7 0.0 reduce-scatter.2.cloned.1.call-start
  14.8 6.1 %copy.16 = bf16[128,14336]{0,1:T(8,128)(2,1)} copy(bf16[128,14336]{1,0:T(8,128)(2,1)} %param.11) | data formatting | bytes 7340032 | tf_op args[5]
  20.8 64.3 %all_to_all.38 = bf16[128,16,896]{0,2,1:T(8,128)(2,1)} all-to-all(bf16[128,16,896]{0,2,1:T(8,128)(2,1)} %bitcast.19), channel_id=1, replica_groups=mesh['rep'=8,'grp'=16] {'grp'}, dimensions={1} | all-to-all | bytes 7340032 | tf_op jit(solution)/shard_map/all_to_all | solution.py:38
  85.2 6.0 %copy.17 = bf16[16,128,896]{2,1,0:T(8,128)(2,1)} copy(bf16[16,128,896]{1,2,0:T(8,128)(2,1)} %bitcast.16) | data formatting | bytes 7340032 | tf_op jit(solution)/shard_map/all_to_all | solution.py:38
  91.2 67.1 %all-gather.3.cloned.1.call-done = bf16[2048,4096]{1,0:T(8,128)(2,1)} async-done(((bf16[128,4096]{1,0:T(8,128)(2,1)}), bf16[2048,4096]{1,0:T(8,128)(2,1)}) %all-gather.3.cloned.1.call-update) | async-done | bytes 16777232 | tf_op jit(solution)/shard_map/all_gather | solution.py:40
  158.3 22.9 %convolution_convert_fusion = bf16[4096,896]{1,0:T(8,128)(2,1)} fusion(bf16[2048,4096]{1,0:T(8,128)(2,1)} %all-gather.3.cloned.1.call-done, bf16[2048,896]{1,0:T(8,128)(2,1)} %bitcast.20), kind=kOutput, calls=%fused_computation | convolution fusion | flops 15036055552 | bytes 27787264 | tf_op jit(solution)/shard_map/dot_general | solution.py:28
  181.3 0.0 reduce-scatter.2.cloned.1.call-update
  181.3 58.9 %all-gather.5.cloned.1.call-done = bf16[4096,896]{1,0:T(8,128)(2,1)} async-done(((bf16[512,896]{1,0:T(8,128)(2,1)}), bf16[4096,896]{1,0:T(8,128)(2,1)}) %all-gather.5.cloned.1.call-update) | async-done | bytes 7340048 | tf_op jit(solution)/shard_map/all_gather | solution.py:39
  240.2 20.4 %convert_bitcast_fusion = bf16[112,16,8,128]{3,2,1,0:T(8,128)(2,1)S(1)} fusion(bf16[4096,896]{1,0:T(8,128)(2,1)} %all-gather.5.cloned.1.call-done, bf16[2048,4096]{1,0:T(8,128)(2,1)} %all-gather.3.cloned.1.call-done), kind=kOutput, calls=%fused_computation.2 | convolution fusion | flops 15034220544 | bytes 27787264 | tf_op jit(solution)/shard_map/dot_general | solution.py:41
  260.6 0.9 copy.22
  261.6 92.1 %all_to_all.39 = bf16[16,128,896]{1,2,0:T(8,128)(2,1)} all-to-all(bf16[16,128,896]{1,2,0:T(8,128)(2,1)S(1)} %bitcast.17), channel_id=1, replica_groups=mesh['rep'=8,'grp'=16] {'grp'}, dimensions={0} | all-to-all | bytes 7340032 | tf_op jit(solution)/shard_map/all_to_all | solution.py:50
  353.7 6.1 %copy.19 = bf16[128,14336]{1,0:T(8,128)(2,1)} copy(bf16[128,14336]{0,1:T(8,128)(2,1)} %bitcast.18) | data formatting | bytes 7340032
  359.8 3.9 %reduce-scatter.2.cloned.1.call-done = bf16[512,896]{1,0:T(8,128)(2,1)} async-done(((bf16[4096,896]{1,0:T(8,128)(2,1)}), bf16[512,896]{1,0:T(8,128)(2,1)}) %reduce-scatter.2.cloned.1.call-update) | async-done | bytes 917520 | tf_op jit(solution)/shard_map/reduce_scatter | solution.py:44
  363.7 2.5 convert_element_type.16
Async XLA Ops:
  7.2 151.2 %all-gather.3.cloned.1.call-start = ((), (), s32[]{:S(2)}) async-start(), calls=%async_computation.3 | async-start | bytes 17825792 | tf_op jit(solution)/shard_map/all_gather | solution.py:40
  7.9 232.3 %all-gather.5.cloned.1.call-start = ((), (), s32[]{:S(2)}) async-start(), calls=%async_computation.5 | async-start | bytes 8257536 | tf_op jit(solution)/shard_map/all_gather | solution.py:39
  14.7 348.9 %reduce-scatter.2.cloned.1.call-start = ((), (), s32[]{:S(2)}) async-start(), calls=%async_computation.4 | async-start | bytes 8257536 | tf_op jit(solution)/shard_map/reduce_scatter | solution.py:44
Sparse Core Ops, SparseCore 0:
  10.5 147.8 all-gather.2
  160.6 79.6 all-gather.4
  242.6 120.9 reduce-scatter.1
where the time goes:
time: 373 us
  blocking collectives  156 us (42%)
  waiting for transfers between devices  131 us (35%)
  matrix products  43.3 us (12%)
  local copies, waits for them, and re-layouts  19.1 us (5%)
  between operations  13.8 us (4%)
  other arithmetic  9.3 us (2%)
    all_to_all x1, blocking collectives, body(): lax.all_to_all(up_columns, 'grp', split_axis=0, concat_axis=1, tiled=True)  92.1 us
    all_gather x1, waiting for transfers between devices, body(): group_tokens = lax.all_gather(tokens, 'grp', axis=0, tiled=True)  67.1 us
    all_to_all x1, blocking collectives, body(): lax.all_to_all(cotangent, 'grp', split_axis=1, concat_axis=0, tiled=True)  64.3 us
    all_gather x1, waiting for transfers between devices, body(): weight_columns = lax.all_gather(weight_half, 'rep', axis=0, tiled=True)  58.9 us
    dot_general x1, matrix products, column_term(): lax.dot_general(group_tokens, back_columns, contract_rows, preferred_elem...  22.9 us
    dot_general x1, matrix products, body(): jnp.dot(group_tokens, weight_columns, preferred_element_type=jnp.float32)  20.4 us
    unnamed x2, local copies, waits for them, and re-layouts  12.1 us
  transfers between devices with their start and end apart: 3, of which 3 were waited for; matrix products, arithmetic and copies ran while one was open for 19% of the time, Pallas kernels for 0%

commit v1 on v0

v1 whole, which is shorter than its diff:
```python
import functools

import jax
import jax.numpy as jnp
from jax import lax
from jax.experimental import pallas as pl
from jax.experimental.pallas import tpu as pltpu
from jax.sharding import PartitionSpec as P

STEP = 100

learning_rate = 0.002
beta_one = 0.9
beta_two = 0.95
epsilon = 1e-08
decay_weight = 0.1

MESH = pl.DeviceIdType.MESH
BF16, F32 = jnp.bfloat16, jnp.float32

ROWS = 128
WIDE = 4096
COLS = 896
PIECE = 512
PAIR = 2 * ROWS
GROUP = 16 * ROWS
QUARTER = 2 * PIECE
TILE = 256

PARTNERS = sorted(
    [(dy, dx, dc) for dy in range(4) for dx in range(2) for dc in range(2) if (dy, dx, dc) != (0, 0, 0)],
    key=lambda t: (-(min(t[0], 4 - t[0]) + 2 * t[1]), t),
)


def adam_update(master_weight, first_moment, second_moment, prior_grad):
    first_new = beta_one * first_moment + (1.0 - beta_one) * prior_grad
    second_new = beta_two * second_moment + (1.0 - beta_two) * prior_grad * prior_grad
    bias_one = 1.0 - beta_one**STEP
    bias_two = 1.0 - beta_two**STEP
    step_size = first_new / bias_one / (jnp.sqrt(second_new / bias_two) + epsilon)
    new_master = master_weight - learning_rate * (step_size + decay_weight * master_weight)
    return (new_master, first_new, second_new)


def kernel(
    w_in, tok_in, cot_in, grad_out, up_out,
    tok, wts, cot, acc, up, gsend, relay_in, zin, xsend, xin, gown,
    loc, cot_s, cot_r, out_s, out_r, tx_s, tx_r, ty_s, ty_r, tr_s, tr_r, ts_s, ts_r,
    wx_s, wx_r, wz_s, wz_r, wr_s, wr_r, g0_s, g0_r, gz_s, gz_r, gx_s, gx_r,
):
    rep, grp = lax.axis_index("rep"), lax.axis_index("grp")
    xl, z = rep // 4, rep % 4
    y, xh, c = grp // 4, (grp // 2) % 2, grp % 2

    def in_group(dy, dx, dc):
        return (rep, ((y + dy) % 4) * 4 + ((xh + dx) % 2) * 2 + (c + dc) % 2)

    def in_rep(dxl, dz):
        return (((xl + dxl) % 2) * 4 + (z + dz) % 4, grp)

    def rows_of(core, yy, half):
        return pl.multiple_of(((core * 4 + yy) * 2 + half) * ROWS, ROWS)

    sends = []

    def send(src, dst, ss, rs, to):
        copy = pltpu.make_async_remote_copy(src, dst, ss, rs, device_id=to, device_id_type=MESH)
        copy.start()
        sends.append(copy)

    def arrived(ref, rs):
        pltpu.make_async_remote_copy(ref, ref, rs, rs, device_id=in_group(0, 0, 1), device_id_type=MESH).wait_recv()

    barrier = pltpu.get_barrier_semaphore()
    peers = [in_group(*t) for t in PARTNERS] + [in_rep(0, 1), in_rep(0, 3), in_rep(1, 0)]
    for peer in peers:
        pl.semaphore_signal(barrier, inc=1, device_id=peer, device_id_type=MESH)
    pl.semaphore_wait(barrier, len(peers))

    own_rows = rows_of(c, y, xh)
    other_rows = rows_of(c, y, 1 - xh)
    places = [
        ((0, (z + 2) % 4), (1, (z + 2) % 4)),
        ((0, (z + 1) % 4), (0, (z + 3) % 4)),
        ((1, (z + 1) % 4), (1, (z + 3) % 4)),
        ((0, z), (1, z)),
    ]
    locals_ = {}
    for q in range(4):
        for h in range(2):
            a, zz = places[q][h]
            first = pl.multiple_of((a * 4 + zz) * PIECE, PIECE)
            locals_[q, h] = pltpu.make_async_copy(
                tok_in.at[:, pl.ds(first, PIECE)],
                tok.at[q, pl.ds(own_rows, ROWS), pl.ds(h * PIECE, PIECE)],
                loc.at[2 * q + h],
            )
            locals_[q, h].start()
    mine = pl.ds(pl.multiple_of(grp * COLS, 128), COLS)
    own_cot = pltpu.make_async_copy(cot_in.at[:, mine], cot.at[pl.ds(own_rows, ROWS)], loc.at[8])
    own_cot.start()
    own_w = pltpu.make_async_copy(
        w_in, wts.at[3, pl.ds(pl.multiple_of(xl * PIECE, PIECE), PIECE)], loc.at[9]
    )
    own_w.start()

    def exchange(q):
        locals_[q, 0].wait()
        locals_[q, 1].wait()
        own = tok.at[q, pl.ds(own_rows, ROWS)]
        send(own, own, tx_s.at[q], tx_r.at[q], in_group(0, 1, 0))

    exchange(0)

    def spread(order, block):
        src = wts.at[3, pl.ds(pl.multiple_of(block * PIECE, PIECE), PIECE)] if order else w_in
        send(src, wts.at[1 + block, pl.ds(PIECE, PIECE)], wz_s.at[order, 0], wz_r.at[order, 0], in_rep(0, 1))
        send(src, wts.at[1 + block, pl.ds(0, PIECE)], wz_s.at[order, 1], wz_r.at[order, 1], in_rep(0, 3))

    send(
        w_in, wts.at[3, pl.ds(pl.multiple_of(xl * PIECE, PIECE), PIECE)], wx_s.at[0], wx_r.at[0], in_rep(1, 0)
    )
    spread(0, xl)

    for i, t in enumerate(PARTNERS):
        to = in_group(*t)
        theirs = pl.ds(pl.multiple_of(to[1] * COLS, 128), COLS)
        send(cot_in.at[:, theirs], cot.at[pl.ds(own_rows, ROWS)], cot_s.at[i], cot_r.at[i], to)

    def pair_rows(core, dy):
        return pl.ds(rows_of(core, (y + dy) % 4, 0), PAIR)

    def half_rows(core, dy, half):
        return pl.ds(rows_of(core, (y + dy) % 4, half), ROWS)

    def to_sibling(q, rows, i):
        block = tok.at[q, rows]
        send(block, block, ts_s.at[q, i], ts_r.at[q, i], in_group(0, 0, 1))

    def step_a(q):
        arrived(tok.at[q, pl.ds(other_rows, ROWS)], tx_r.at[q])
        rows = pair_rows(c, 0)
        pair = tok.at[q, rows]
        send(pair, pair, ty_s.at[q, 0], ty_r.at[q, 0], in_group(1, 0, 0))
        send(pair, pair, ty_s.at[q, 1], ty_r.at[q, 1], in_group(3, 0, 0))
        to_sibling(q, rows, 0)

    def step_b(q):
        arrived(tok.at[q, pair_rows(c, 3)], ty_r.at[q, 0])
        onward = tok.at[q, half_rows(c, 3, 0)]
        send(onward, onward, tr_s.at[q, 0], tr_r.at[q, 0], in_group(1, 0, 0))
        arrived(tok.at[q, pair_rows(c, 1)], ty_r.at[q, 1])
        onward = tok.at[q, half_rows(c, 1, 1)]
        send(onward, onward, tr_s.at[q, 1], tr_r.at[q, 1], in_group(3, 0, 0))
        to_sibling(q, pair_rows(c, 3), 1)
        to_sibling(q, pair_rows(c, 1), 2)

    def step_c(q):
        for half in range(2):
            arrived(tok.at[q, half_rows(c, 2, half)], tr_r.at[q, half])
            to_sibling(q, half_rows(c, 2, half), 3 + half)

    def gathered(q):
        arrived(tok.at[q, pair_rows(1 - c, 0)], ts_r.at[q, 0])
        arrived(tok.at[q, pair_rows(1 - c, 3)], ts_r.at[q, 1])
        arrived(tok.at[q, pair_rows(1 - c, 1)], ts_r.at[q, 2])
        arrived(tok.at[q, half_rows(1 - c, 2, 0)], ts_r.at[q, 3])
        arrived(tok.at[q, half_rows(1 - c, 2, 1)], ts_r.at[q, 4])

    def weight_second():
        arrived(wts.at[3, pl.ds(pl.multiple_of((1 - xl) * PIECE, PIECE), PIECE)], wx_r.at[0])
        spread(1, 1 - xl)

    def weight_up():
        src = wts.at[1 + xl, pl.ds(PIECE, PIECE)]
        arrived(src, wz_r.at[0, 0])
        send(
            src, wts.at[0, pl.ds(pl.multiple_of(xl * PIECE, PIECE), PIECE)], wr_s.at[0], wr_r.at[0], in_rep(0, 1)
        )

    def weight_down():
        src = wts.at[2 - xl, pl.ds(0, PIECE)]
        arrived(src, wz_r.at[1, 1])
        send(
            src,
            wts.at[0, pl.ds(pl.multiple_of((1 - xl) * PIECE, PIECE), PIECE)],
            wr_s.at[1],
            wr_r.at[1],
            in_rep(0, 3),
        )

    def weight_rest():
        arrived(wts.at[1 + xl, pl.ds(0, PIECE)], wz_r.at[0, 1])
        arrived(wts.at[2 - xl, pl.ds(PIECE, PIECE)], wz_r.at[1, 0])
        arrived(wts.at[0, pl.ds(pl.multiple_of(xl * PIECE, PIECE), PIECE)], wr_r.at[0])
        arrived(wts.at[0, pl.ds(pl.multiple_of((1 - xl) * PIECE, PIECE), PIECE)], wr_r.at[1])
        own_w.wait()

    def grad_tile(q, first):
        return lax.dot_general(
            tok[q, :, pl.ds(first, TILE)], cot[...], (((0,), (0,)), ((), ())), preferred_element_type=F32
        )

    def grad_half(q, h, add=None):
        def tile(m, carry):
            here = pl.ds(pl.multiple_of(m * TILE, TILE), TILE)
            value = grad_tile(q, pl.multiple_of(h * PIECE + m * TILE, TILE))
            if add is not None:
                value = value + add[here, :].astype(F32)
            gsend[q, pl.ds(pl.multiple_of(h * PIECE + m * TILE, TILE), TILE), :] = value.astype(BF16)
            return carry

        lax.fori_loop(0, PIECE // TILE, tile, 0)

    def grad_zero():
        grad_half(0, 0)
        send(gsend.at[0, pl.ds(0, PIECE)], relay_in.at[0], g0_s.at[0], g0_r.at[0], in_rep(0, 1))
        grad_half(0, 1)
        send(gsend.at[0, pl.ds(PIECE, PIECE)], relay_in.at[1], g0_s.at[1], g0_r.at[1], in_rep(0, 3))

    def grad_neighbours(q):
        a = q - 1
        relayed = relay_in.at[a]

        def part(h):
            add = None
            if h == a:
                arrived(relayed, g0_r.at[a])
                add = relayed
            grad_half(q, h, add)
            send(
                gsend.at[q, pl.ds(h * PIECE, PIECE)],
                zin.at[a, h],
                gz_s.at[a, h],
                gz_r.at[a, h],
                in_rep(0, 3 if h else 1),
            )

        part(1 - a)
        part(a)

    def forward(q, last=False):
        def block(rows):
            value = jnp.dot(tok[q, rows, :], wts[q], preferred_element_type=F32)
            if q:
                value = value + acc[rows, :]
            if last:
                up[rows, :] = value.astype(BF16)
            else:
                acc[rows, :] = value

        def step(i, carry):
            block(pl.ds(pl.multiple_of(i * PAIR, PAIR), PAIR))
            return carry

        if not last:
            lax.fori_loop(0, GROUP // PAIR, step, 0)
            return
        for dy in (2, 1, 3, 0):
            for dc in range(2):
                core = (c + dc) % 2
                block(pair_rows(core, dy))
                for dx in (1, 0):
                    src = up.at[half_rows(core, dy, (xh + dx) % 2)]
                    if (dy, dx, dc) == (0, 0, 0):
                        own_up = pltpu.make_async_copy(src, up_out.at[:, mine], loc.at[10])
                        own_up.start()
                        locals_["up"] = own_up
                        continue
                    i = PARTNERS.index((dy, dx, dc))
                    send(src, up_out.at[:, mine], out_s.at[i], out_r.at[i], in_group(dy, dx, dc))

    def cotangent_here():
        own_cot.wait()
        for i, (dy, dx, dc) in enumerate(PARTNERS):
            place = pl.ds(rows_of((c - dc) % 2, (y - dy) % 4, (xh - dx) % 2), ROWS)
            arrived(cot.at[place], cot_r.at[i])

    exchange(1)
    step_a(0)
    exchange(2)
    weight_second()
    step_a(1)
    step_b(0)
    exchange(3)
    weight_up()
    step_a(2)
    step_b(1)
    step_c(0)
    weight_down()
    cotangent_here()
    gathered(0)
    grad_zero()
    step_a(3)
    step_b(2)
    step_c(1)
    weight_rest()
    forward(0)
    gathered(1)
    grad_neighbours(1)
    step_b(3)
    step_c(2)
    forward(1)
    gathered(2)
    grad_neighbours(2)
    step_c(3)
    forward(2)
    gathered(3)
    forward(3, last=True)

    def closing(a, store):
        def tile(m, carry):
            here = pl.ds(pl.multiple_of(m * TILE, TILE), TILE)
            value = grad_tile(3, pl.multiple_of(a * PIECE + m * TILE, TILE))
            value = value + zin[a, 0, here, :].astype(F32) + zin[a, 1, here, :].astype(F32)
            store(here, value)
            return carry

        lax.fori_loop(0, PIECE // TILE, tile, 0)

    def to_partner(here, value):
        xsend[here, :] = value.astype(BF16)

    def to_own(here, value):
        gown[here, :] = value

    for a in range(2):
        for h in range(2):
            arrived(zin.at[a, h], gz_r.at[a, h])
    closing(1 - xl, to_partner)
    send(xsend, xin, gx_s.at[0], gx_r.at[0], in_rep(1, 0))
    closing(xl, to_own)
    arrived(xin, gx_r.at[0])
    gown[...] = gown[...] + xin[...].astype(F32)
    result = pltpu.make_async_copy(gown, grad_out, loc.at[11])
    result.start()
    result.wait()
    for i, (dy, dx, dc) in enumerate(PARTNERS):
        source = ((y - dy) % 4) * 4 + ((xh - dx) % 2) * 2 + (c - dc) % 2
        arrived(up_out.at[:, pl.ds(pl.multiple_of(source * COLS, 128), COLS)], out_r.at[i])
    locals_["up"].wait()
    for copy in sends:
        copy.wait_send()


def exchange_and_multiply(weight_half, tokens, cotangent):
    dma = pltpu.SemaphoreType.DMA
    n = len(PARTNERS)
    return pl.pallas_call(
        kernel,
        out_shape=(
            jax.ShapeDtypeStruct((PIECE, COLS), F32),
            jax.ShapeDtypeStruct((ROWS, 16 * COLS), BF16),
        ),
        in_specs=[pl.BlockSpec(memory_space=pl.ANY)] * 3,
        out_specs=(pl.BlockSpec(memory_space=pl.ANY),) * 2,
        scratch_shapes=[
            pltpu.VMEM((4, GROUP, QUARTER), BF16),
            pltpu.VMEM((4, QUARTER, COLS), BF16),
            pltpu.VMEM((GROUP, COLS), BF16),
            pltpu.VMEM((GROUP, COLS), F32),
            pltpu.VMEM((GROUP, COLS), BF16),
            pltpu.VMEM((3, QUARTER, COLS), BF16),
            pltpu.VMEM((2, PIECE, COLS), BF16),
            pltpu.VMEM((2, 2, PIECE, COLS), BF16),
            pltpu.VMEM((PIECE, COLS), BF16),
            pltpu.VMEM((PIECE, COLS), BF16),
            pltpu.VMEM((PIECE, COLS), F32),
            dma((12,)),
            dma((n,)), dma((n,)),
            dma((n,)), dma((n,)),
            dma((4,)), dma((4,)),
            dma((4, 2)), dma((4, 2)),
            dma((4, 2)), dma((4, 2)),
            dma((4, 5)), dma((4, 5)),
            dma((1,)), dma((1,)),
            dma((2, 2)), dma((2, 2)),
            dma((2,)), dma((2,)),
            dma((2,)), dma((2,)),
            dma((2, 2)), dma((2, 2)),
            dma((1,)), dma((1,)),
        ],
        compiler_params=pltpu.CompilerParams(
            collective_id=0, has_side_effects=True, vmem_limit_bytes=62 * 2**20
        ),
        cost_estimate=pl.CostEstimate(
            flops=4 * GROUP * WIDE * COLS, bytes_accessed=16 * 2**20, transcendentals=0
        ),
        name="exchange_and_multiply",
    )(weight_half, tokens, cotangent)


def body(master_weight, first_moment, second_moment, prior_grad, tokens, cotangent):
    new_master, first_new, second_new = adam_update(
        master_weight, first_moment, second_moment, prior_grad
    )
    weight_half = new_master.astype(BF16)
    grad_sum, up_proj = exchange_and_multiply(weight_half, tokens, cotangent)
    return (new_master, first_new, second_new, grad_sum, up_proj)


def solution(mesh):
    return jax.shard_map(
        body,
        mesh=mesh,
        in_specs=(
            P("rep", "grp"),
            P("rep", "grp"),
            P("rep", "grp"),
            P("rep", "grp"),
            P(("rep", "grp"), None),
            P(("rep", "grp"), None),
        ),
        out_specs=(
            P("rep", "grp"),
            P("rep", "grp"),
            P("rep", "grp"),
            P("rep", "grp"),
            P(("rep", "grp"), None),
        ),
        check_vma=False,
    )
```

time: 373 us -> 225 us (0.60)
  Pallas kernels: 0 us -> 210 us
  blocking collectives: 156 us -> 0 us
  waiting for transfers between devices: 131 us -> 0 us
  matrix products: 43.3 us -> 0 us
  local copies, waits for them, and re-layouts: 19.1 us -> 4.84 us
  between operations: 13.8 us -> 0.65 us
    pallas_call x0 -> x1, Pallas kernels: none -> 210 us  [exchange_and_multiply(): pl.pallas_call(kernel, out_shape=(jax.ShapeDtypeStruct((PIECE, COLS), F32...]
    all_to_all x2 -> x0, blocking collectives: 156 us -> none  [the longest x1 92.1 us: body(): lax.all_to_all(up_columns, 'grp', split_axis=0, concat_axis=1, tiled=True)]
    all_gather x2 -> x0, waiting for transfers between devices: 126 us -> none  [the longest x1 67.1 us: body(): group_tokens = lax.all_gather(tokens, 'grp', axis=0, tiled=True)]
    dot_general x2 -> x0, matrix products: 43.3 us -> none  [the longest x1 22.9 us: column_term(): lax.dot_general(group_tokens, back_columns, contract_rows, preferred_elem...]
    unnamed x2 -> x4, local copies, waits for them, and re-layouts: 12.1 us -> 4.84 us
    all_to_all x2 -> x0, local copies, waits for them, and re-layouts: 6.99 us -> none  [the longest x1 6.05 us: body(): lax.all_to_all(cotangent, 'grp', split_axis=1, concat_axis=0, tiled=True)]
    reduce_scatter x1 -> x0, waiting for transfers between devices: 3.86 us -> none  [body(): lax.psum_scatter(column_term(group_tokens, back_columns).astype(jnp.bfloa...]
    convert_element_type x2 -> x1, other arithmetic: 9.3 us -> 6.77 us  [body(): weight_half = new_master.astype(BF16)]
  transfers between devices with their start and end apart: 3 -> 0, of which waited for: 3 -> 0; matrix products, arithmetic and copies ran while one was open for 19% -> 0% of each run, Pallas kernels for 0% -> 0%
where the time goes in v1:
time: 225 us; the launch traced here: 223 us
  Pallas kernels  210 us (93%)
  other arithmetic  6.77 us (3%)
  local copies, waits for them, and re-layouts  4.84 us (2%)
    pallas_call x1, Pallas kernels, exchange_and_multiply(): pl.pallas_call(kernel, out_shape=(jax.ShapeDtypeStruct((PIECE, COLS), F32...  210 us
    convert_element_type x1, other arithmetic, body(): weight_half = new_master.astype(BF16)  6.77 us
    unnamed x4, local copies, waits for them, and re-layouts  4.84 us

profile of v1, /device:TPU:1, one launch (start us, length us, event | category | flops | bytes accessed | tf_op | source)
XLA Modules:
  0.0 222.7 jit_solution(17776173169979978528)
XLA Ops:
  0.6 6.8 %fusion.1 = (bf16[512,896]{1,0:T(8,128)(2,1)}, f32[512,896]{1,0:T(8,128)}, f32[512,896]{1,0:T(8,128)}, f32[512,896]{1,0:T(8,128)}) fusion(f32[512,896]{1,0:T(8,128)} %param.6, f32[512,896]{1,0:T(8,128)} %param.9, f32[512,896]{1,0:T(8,128)} %param.7, f32[512,896]{1,0:T(8,128)} %param.8), kind=kLoop, calls=%fused_computation.4 | loop fusion | flops 7340032 | bytes 13762560 | tf_op jit(solution)/shard_map/convert_element_type | solution.py:398
  7.4 210.5 %exchange_and_multiply.1 = (f32[512,896]{1,0:T(8,128)}, bf16[128,14336]{1,0:T(8,128)(2,1)}) custom-call(bf16[512,896]{1,0:T(8,128)(2,1)} %get-tuple-element.9.w_in, bf16[128,4096]{1,0:T(8,128)(2,1)} %tok_in.1, bf16[128,14336]{1,0:T(8,128)(2,1)} %cot_in.1), custom_call_target="tpu_custom_call" | custom-call | flops 30064771072 | bytes 16777216 | tf_op jit(solution)/shard_map/exchange_and_multiply/pallas_call | solution.py:350
  217.9 0.0 copy-start
  217.9 3.0 %copy.13 = f32[512,896]{1,0:T(8,128)} copy(f32[512,896]{1,0:T(8,128)} %get-tuple-element.21) | data formatting | bytes 3670016
  220.9 0.0 copy-done
  220.9 1.8 copy.14
Async XLA Ops:
  217.9 3.0 %copy-start = (bf16[128,14336]{1,0:T(8,128)(2,1)S(1)}, bf16[128,14336]{1,0:T(8,128)(2,1)}, u32[]{:S(2)}) copy-start(bf16[128,14336]{1,0:T(8,128)(2,1)} %get-tuple-element.22) | copy-start | bytes 11010052

commit v2 on v0

v2 whole, which is shorter than its diff:
```python
import jax
import jax.numpy as jnp
from jax import lax
from jax.experimental import pallas as pl
from jax.experimental.pallas import tpu as pltpu
from jax.sharding import PartitionSpec as P

STEP = 100

learning_rate = 0.002
beta_one = 0.9
beta_two = 0.95
epsilon = 1e-08
decay_weight = 0.1

MESH = pl.DeviceIdType.MESH
BF16, F32 = jnp.bfloat16, jnp.float32

ROWS = 128
WIDE = 4096
COLS = 896
PIECE = 512
HALF = 256
PAIR = 2 * ROWS
GROUP = 16 * ROWS
QUARTER = 1024

PARTNERS = sorted(
    [(dy, dx, dc) for dy in range(4) for dx in range(2) for dc in range(2) if (dy, dx, dc) != (0, 0, 0)],
    key=lambda t: (-(min(t[0], 4 - t[0]) + 2 * t[1]), t),
)

SCHEDULE = (
    ("cotangent_far", 2),
    ("exchange", 2),
    ("cotangent_near",),
    ("exchange", 0),
    ("weight_across",),
    ("exchange", 1),
    ("weight_own",),
    ("cotangent_far", 3),
    ("weight_relay", 0),
    ("pair", 0),
    ("cotangent_far", 1),
    ("cotangent_far", 0),
    ("exchange", 3),
    ("pair", 2),
    ("gathered_own", 2),
    ("relay", 0),
    ("weight_second",),
    ("relay", 2),
    ("pair", 1),
    ("weight_relay", 1),
    ("share", 0),
    ("cotangent_wait",),
    ("weight_wait",),
    ("gathered_own", 0),
    ("gathered", 0),
    ("gradient", 0, 1),
    ("share", 2),
    ("gradient", 0, 0),
    ("pair", 3),
    ("gathered_own", 1),
    ("gathered", 2),
    ("gradient", 2, 0),
    ("forward", 0),
    ("gathered_own", 3),
    ("relay", 1),
    ("forward_own",),
    ("relay", 3),
    ("forward", 2),
    ("share", 1),
    ("gradient", 2, 1),
    ("gathered", 1),
    ("forward", 1),
    ("share", 3),
    ("gathered", 3),
    ("forward_last", 3),
    ("forward_last", 2),
    ("forward_last", 1),
    ("gradient", 1, 1),
    ("gradient", 1, 0),
    ("closing", 1),
    ("closing", 0),
)


def adam_update(master_weight, first_moment, second_moment, prior_grad):
    first_new = beta_one * first_moment + (1.0 - beta_one) * prior_grad
    second_new = beta_two * second_moment + (1.0 - beta_two) * prior_grad * prior_grad
    bias_one = 1.0 - beta_one**STEP
    bias_two = 1.0 - beta_two**STEP
    step_size = first_new / bias_one / (jnp.sqrt(second_new / bias_two) + epsilon)
    new_master = master_weight - learning_rate * (step_size + decay_weight * master_weight)
    return (new_master, first_new, second_new)


def kernel(
    w_in, tok_in, cot_in, grad_out, up_out,
    tok, wts, cot, acc, up, gsend, relay_in, zin, xsend, xin, gown,
    own_t, own_c, own_w, own_u, own_g,
    cot_s, cot_r, out_s, out_r, tx_s, tx_r, ty_s, ty_r, tr_s, tr_r, ts_s, ts_r,
    wx_s, wx_r, wz_s, wz_r, wr_s, wr_r, g0_s, g0_r, gz_s, gz_r, gx_s, gx_r,
):
    rep, grp = lax.axis_index("rep"), lax.axis_index("grp")
    xl, z = rep // 4, rep % 4
    y, xh, c = grp // 4, (grp // 2) % 2, grp % 2

    def in_group(dy, dx, dc):
        return (rep, ((y + dy) % 4) * 4 + ((xh + dx) % 2) * 2 + (c + dc) % 2)

    def in_rep(dxl, dz):
        return (((xl + dxl) % 2) * 4 + (z + dz) % 4, grp)

    sends = []

    def send(src, dst, ss, rs, to):
        copy = pltpu.make_async_remote_copy(src, dst, ss, rs, device_id=to, device_id_type=MESH)
        copy.start()
        sends.append(copy)

    def arrived(ref, rs):
        pltpu.make_async_remote_copy(
            ref, ref, rs, rs, device_id=in_group(0, 0, 1), device_id_type=MESH
        ).wait_recv()

    def row(core, dy, half):
        return pl.multiple_of(((core * 4 + (y + dy) % 4) * 2 + half) * ROWS, ROWS)

    def block_rows(core, dy, half):
        return pl.ds(row(core, dy, half), ROWS)

    def pair_rows(core, dy):
        return pl.ds(row(core, dy, 0), PAIR)

    def columns(device):
        return pl.ds(pl.multiple_of(device * COLS, 128), COLS)

    barrier = pltpu.get_barrier_semaphore()
    peers = [in_group(*t) for t in PARTNERS] + [in_rep(0, 1), in_rep(0, 3), in_rep(1, 0)]
    for peer in peers:
        pl.semaphore_signal(barrier, inc=1, device_id=peer, device_id_type=MESH)
    pl.semaphore_wait(barrier, len(peers))

    own = block_rows(c, 0, xh)
    own_tokens = {}
    for q in range(4):
        for h in range(2):
            zz = (z + (2, 1, 1, 0)[q] + (2 * h if q in (1, 2) else 0)) % 4
            hh = (h, 0, 1, h)[q]
            for a in range(2):
                copy = pltpu.make_async_copy(
                    tok_in.at[:, pl.ds(pl.multiple_of((a * 4 + zz) * PIECE + hh * HALF, HALF), HALF)],
                    tok.at[q, own, pl.ds(h * PIECE + a * HALF, HALF)],
                    own_t.at[q, 2 * h + a],
                )
                copy.start()
                own_tokens[q, h, a] = copy
    own_cot = pltpu.make_async_copy(cot_in.at[:, columns(grp)], cot.at[own], own_c.at[0])
    own_cot.start()
    own_weight = pltpu.make_async_copy(w_in, wts.at[3, :, xl], own_w.at[0])
    own_weight.start()
    own_up = pltpu.make_async_copy(up.at[own], up_out.at[:, columns(grp)], own_u.at[0])
    own_grad = [
        pltpu.make_async_copy(
            gown.at[pl.ds(h * HALF, HALF)], grad_out.at[pl.ds(h * HALF, HALF)], own_g.at[h]
        )
        for h in range(2)
    ]

    def to_sibling(q, rows, i):
        block = tok.at[q, rows]
        send(block, block, ts_s.at[q, i], ts_r.at[q, i], in_group(0, 0, 1))

    def exchange(q):
        for h in range(2):
            for a in range(2):
                own_tokens[q, h, a].wait()
        block = tok.at[q, own]
        send(block, block, tx_s.at[q], tx_r.at[q], in_group(0, 1, 0))

    def pair(q):
        arrived(tok.at[q, block_rows(c, 0, 1 - xh)], tx_r.at[q])
        block = tok.at[q, pair_rows(c, 0)]
        send(block, block, ty_s.at[q, 0], ty_r.at[q, 0], in_group(1, 0, 0))
        send(block, block, ty_s.at[q, 1], ty_r.at[q, 1], in_group(3, 0, 0))
        to_sibling(q, pair_rows(c, 0), 0)

    def relay(q):
        for i, back, to in ((0, 3, 1), (1, 1, 3)):
            arrived(tok.at[q, pair_rows(c, back)], ty_r.at[q, i])
            onward = tok.at[q, block_rows(c, back, i)]
            send(onward, onward, tr_s.at[q, i], tr_r.at[q, i], in_group(to, 0, 0))
        to_sibling(q, pair_rows(c, 3), 1)
        to_sibling(q, pair_rows(c, 1), 2)

    def share(q):
        for i in range(2):
            arrived(tok.at[q, block_rows(c, 2, i)], tr_r.at[q, i])
            to_sibling(q, block_rows(c, 2, i), 3 + i)

    def gathered_own(q):
        arrived(tok.at[q, pair_rows(1 - c, 0)], ts_r.at[q, 0])

    def gathered(q):
        for i, dy in ((1, 3), (2, 1)):
            arrived(tok.at[q, pair_rows(1 - c, dy)], ts_r.at[q, i])
        for i in range(2):
            arrived(tok.at[q, block_rows(1 - c, 2, i)], ts_r.at[q, 3 + i])

    def cotangent_to(i):
        to = in_group(*PARTNERS[i])
        send(cot_in.at[:, columns(to[1])], cot.at[own], cot_s.at[i], cot_r.at[i], to)

    def cotangent_near():
        for i, (dy, dx, dc) in enumerate(PARTNERS):
            if not dx:
                cotangent_to(i)

    def cotangent_far(far):
        for i, (dy, dx, dc) in enumerate(PARTNERS):
            if dx and dy == far:
                cotangent_to(i)

    def cotangent_wait():
        own_cot.wait()
        for i, (dy, dx, dc) in enumerate(PARTNERS):
            arrived(cot.at[block_rows((c - dc) % 2, -dy, (xh - dx) % 2)], cot_r.at[i])

    def spread(order, a):
        src = wts.at[3, :, a] if order else w_in
        send(src, wts.at[pl.ds(1, 2), 1, a], wz_s.at[order, 0], wz_r.at[order, 0], in_rep(0, 1))
        send(src, wts.at[pl.ds(1, 2), 0, a], wz_s.at[order, 1], wz_r.at[order, 1], in_rep(0, 3))

    def weight_own():
        spread(0, xl)

    def weight_across():
        send(w_in, wts.at[3, :, xl], wx_s.at[0], wx_r.at[0], in_rep(1, 0))

    def weight_second():
        arrived(wts.at[3, :, 1 - xl], wx_r.at[0])
        spread(1, 1 - xl)

    def weight_relay(order):
        a = 1 - xl if order else xl
        arrived(wts.at[pl.ds(1, 2), 1, a], wz_r.at[order, 0])
        send(wts.at[1, 1, a], wts.at[0, 0, a], wr_s.at[order, 0], wr_r.at[order, 0], in_rep(0, 1))
        arrived(wts.at[pl.ds(1, 2), 0, a], wz_r.at[order, 1])
        send(wts.at[2, 0, a], wts.at[0, 1, a], wr_s.at[order, 1], wr_r.at[order, 1], in_rep(0, 3))

    def weight_wait():
        for order in range(2):
            a = 1 - xl if order else xl
            for h in range(2):
                arrived(wts.at[0, h, a], wr_r.at[order, h])
        own_weight.wait()

    def gradient_tile(q, first):
        return lax.dot_general(
            tok[q, :, pl.ds(first, HALF)], cot[...], (((0,), (0,)), ((), ())), preferred_element_type=F32
        )

    def gradient_piece(q, h, add):
        def tile(m, carry):
            first = pl.multiple_of(h * PIECE + m * HALF, HALF)
            value = gradient_tile(q, first)
            if add is not None:
                value = value + add[pl.ds(pl.multiple_of(m * HALF, HALF), HALF), :].astype(F32)
            gsend[q, pl.ds(first, HALF), :] = value.astype(BF16)
            return carry

        lax.fori_loop(0, 2, tile, 0)

    def gradient(q, h):
        relayed = q == h + 1
        if relayed:
            arrived(relay_in.at[h], g0_r.at[h])
        gradient_piece(q, h, relay_in.at[h] if relayed else None)
        src, to = gsend.at[q, pl.ds(h * PIECE, PIECE)], in_rep(0, 3 if h else 1)
        if q:
            send(src, zin.at[q - 1, h], gz_s.at[q - 1, h], gz_r.at[q - 1, h], to)
        else:
            send(src, relay_in.at[h], g0_s.at[h], g0_r.at[h], to)

    def closing_tile(h, a):
        here = pl.ds(pl.multiple_of(a * HALF, HALF), HALF)
        value = gradient_tile(3, pl.multiple_of(h * PIECE + a * HALF, HALF))
        return value + zin[h, 0, here, :].astype(F32) + zin[h, 1, here, :].astype(F32)

    def closing(h):
        for i in range(2):
            arrived(zin.at[h, i], gz_r.at[h, i])
        here = pl.ds(h * HALF, HALF)
        xsend[here, :] = closing_tile(h, 1 - xl).astype(BF16)
        send(xsend.at[here], xin.at[here], gx_s.at[h], gx_r.at[h], in_rep(1, 0))
        gown[here, :] = closing_tile(h, xl)

    def forward_block(q, rows):
        return jnp.dot(tok[q, rows, :], wts[q].reshape(QUARTER, COLS), preferred_element_type=F32)

    def forward(q):
        def block(i, carry):
            rows = pair_rows(i // 3, 1 + i % 3)
            value = forward_block(q, rows)
            acc[rows, :] = value + acc[rows, :] if q else value
            return carry

        lax.fori_loop(0, 6, block, 0)

    def home(dy, dc):
        core = (c + dc) % 2
        for dx in (1, 0):
            if (dy, dx, dc) == (0, 0, 0):
                own_up.start()
                continue
            i = PARTNERS.index((dy, dx, dc))
            src = up.at[block_rows(core, dy, (xh + dx) % 2)]
            send(src, up_out.at[:, columns(grp)], out_s.at[i], out_r.at[i], in_group(dy, dx, dc))

    def forward_own():
        for dc in range(2):
            rows = pair_rows((c + dc) % 2, 0)
            up[rows, :] = sum(forward_block(q, rows) for q in range(4)).astype(BF16)
            home(0, dc)

    def forward_last(dy):
        for dc in range(2):
            rows = pair_rows((c + dc) % 2, dy)
            up[rows, :] = (forward_block(3, rows) + acc[rows, :]).astype(BF16)
            home(dy, dc)

    steps = {
        f.__name__: f
        for f in (
            exchange, pair, relay, share, gathered_own, gathered, cotangent_near, cotangent_far, cotangent_wait,
            weight_own, weight_across, weight_second, weight_relay, weight_wait,
            gradient, forward, forward_own, forward_last, closing,
        )
    }
    for name, *which in SCHEDULE:
        steps[name](*which)

    for h in range(2):
        here = pl.ds(h * HALF, HALF)
        arrived(xin.at[here], gx_r.at[h])
        gown[here, :] = gown[here, :] + xin[here, :].astype(F32)
        own_grad[h].start()
    for i, (dy, dx, dc) in enumerate(PARTNERS):
        source = ((y - dy) % 4) * 4 + ((xh - dx) % 2) * 2 + (c - dc) % 2
        arrived(up_out.at[:, columns(source)], out_r.at[i])
    own_up.wait()
    for copy in own_grad:
        copy.wait()
    for copy in sends:
        copy.wait_send()


def exchange_and_multiply(weight_half, tokens, cotangent):
    dma = pltpu.SemaphoreType.DMA
    n = len(PARTNERS)
    return pl.pallas_call(
        kernel,
        out_shape=(
            jax.ShapeDtypeStruct((PIECE, COLS), F32),
            jax.ShapeDtypeStruct((ROWS, 16 * COLS), BF16),
        ),
        in_specs=[pl.BlockSpec(memory_space=pl.ANY)] * 3,
        out_specs=(pl.BlockSpec(memory_space=pl.ANY),) * 2,
        scratch_shapes=[
            pltpu.VMEM((4, GROUP, QUARTER), BF16),
            pltpu.VMEM((4, 2, 2, HALF, COLS), BF16),
            pltpu.VMEM((GROUP, COLS), BF16),
            pltpu.VMEM((GROUP, COLS), F32),
            pltpu.VMEM((GROUP, COLS), BF16),
            pltpu.VMEM((3, QUARTER, COLS), BF16),
            pltpu.VMEM((2, PIECE, COLS), BF16),
            pltpu.VMEM((2, 2, PIECE, COLS), BF16),
            pltpu.VMEM((PIECE, COLS), BF16),
            pltpu.VMEM((PIECE, COLS), BF16),
            pltpu.VMEM((PIECE, COLS), F32),
            dma((4, 4)), dma((1,)), dma((1,)), dma((1,)), dma((2,)),
            dma((n,)), dma((n,)),
            dma((n,)), dma((n,)),
            dma((4,)), dma((4,)),
            dma((4, 2)), dma((4, 2)),
            dma((4, 2)), dma((4, 2)),
            dma((4, 5)), dma((4, 5)),
            dma((1,)), dma((1,)),
            dma((2, 2)), dma((2, 2)),
            dma((2, 2)), dma((2, 2)),
            dma((2,)), dma((2,)),
            dma((2, 2)), dma((2, 2)),
            dma((2,)), dma((2,)),
        ],
        compiler_params=pltpu.CompilerParams(
            collective_id=0, has_side_effects=True, vmem_limit_bytes=62 * 2**20
        ),
        cost_estimate=pl.CostEstimate(
            flops=4 * GROUP * WIDE * COLS, bytes_accessed=16 * 2**20, transcendentals=0
        ),
        name="exchange_and_multiply",
    )(weight_half.reshape(2, HALF, COLS), tokens, cotangent)


def body(master_weight, first_moment, second_moment, prior_grad, tokens, cotangent):
    new_master, first_new, second_new = adam_update(
        master_weight, first_moment, second_moment, prior_grad
    )
    weight_half = new_master.astype(BF16)
    grad_sum, up_proj = exchange_and_multiply(weight_half, tokens, cotangent)
    return (new_master, first_new, second_new, grad_sum, up_proj)


def solution(mesh):
    return jax.shard_map(
        body,
        mesh=mesh,
        in_specs=(
            P("rep", "grp"),
            P("rep", "grp"),
            P("rep", "grp"),
            P("rep", "grp"),
            P(("rep", "grp"), None),
            P(("rep", "grp"), None),
        ),
        out_specs=(
            P("rep", "grp"),
            P("rep", "grp"),
            P("rep", "grp"),
            P("rep", "grp"),
            P(("rep", "grp"), None),
        ),
        check_vma=False,
    )
```

time: 373 us -> 188 us (0.50)
  Pallas kernels: 0 us -> 176 us
  blocking collectives: 156 us -> 0 us
  waiting for transfers between devices: 131 us -> 0 us
  matrix products: 43.3 us -> 0 us
  local copies, waits for them, and re-layouts: 19.1 us -> 4.84 us
  between operations: 13.8 us -> 0.65 us
    pallas_call x0 -> x1, Pallas kernels: none -> 176 us  [exchange_and_multiply(): pl.pallas_call(kernel, out_shape=(jax.ShapeDtypeStruct((PIECE, COLS), F32...]
    all_to_all x2 -> x0, blocking collectives: 156 us -> none  [the longest x1 92.1 us: body(): lax.all_to_all(up_columns, 'grp', split_axis=0, concat_axis=1, tiled=True)]
    all_gather x2 -> x0, waiting for transfers between devices: 126 us -> none  [the longest x1 67.1 us: body(): group_tokens = lax.all_gather(tokens, 'grp', axis=0, tiled=True)]
    dot_general x2 -> x0, matrix products: 43.3 us -> none  [the longest x1 22.9 us: column_term(): lax.dot_general(group_tokens, back_columns, contract_rows, preferred_elem...]
    unnamed x2 -> x4, local copies, waits for them, and re-layouts: 12.1 us -> 4.84 us
    all_to_all x2 -> x0, local copies, waits for them, and re-layouts: 6.99 us -> none  [the longest x1 6.05 us: body(): lax.all_to_all(cotangent, 'grp', split_axis=1, concat_axis=0, tiled=True)]
    reduce_scatter x1 -> x0, waiting for transfers between devices: 3.86 us -> none  [body(): lax.psum_scatter(column_term(group_tokens, back_columns).astype(jnp.bfloa...]
    convert_element_type x2 -> x1, other arithmetic: 9.3 us -> 6.77 us  [body(): weight_half = new_master.astype(BF16)]
  transfers between devices with their start and end apart: 3 -> 0, of which waited for: 3 -> 0; matrix products, arithmetic and copies ran while one was open for 19% -> 0% of each run, Pallas kernels for 0% -> 0%
where the time goes in v2:
time: 188 us
  Pallas kernels  176 us (94%)
  other arithmetic  6.77 us (4%)
  local copies, waits for them, and re-layouts  4.84 us (3%)
    pallas_call x1, Pallas kernels, exchange_and_multiply(): pl.pallas_call(kernel, out_shape=(jax.ShapeDtypeStruct((PIECE, COLS), F32...  176 us
    convert_element_type x1, other arithmetic, body(): weight_half = new_master.astype(BF16)  6.77 us
    unnamed x4, local copies, waits for them, and re-layouts  4.84 us

profile of v2, /device:TPU:1, one launch (start us, length us, event | category | flops | bytes accessed | tf_op | source)
XLA Modules:
  0.0 188.1 jit_solution(11480391065765485178)
XLA Ops:
  0.6 6.8 %fusion.1 = (bf16[512,896]{1,0:T(8,128)(2,1)}, f32[512,896]{1,0:T(8,128)}, f32[512,896]{1,0:T(8,128)}, f32[512,896]{1,0:T(8,128)}) fusion(f32[512,896]{1,0:T(8,128)} %param.6, f32[512,896]{1,0:T(8,128)} %param.9, f32[512,896]{1,0:T(8,128)} %param.7, f32[512,896]{1,0:T(8,128)} %param.8), kind=kLoop, calls=%fused_computation.4 | loop fusion | flops 7340032 | bytes 13762560 | tf_op jit(solution)/shard_map/convert_element_type | solution.py:410
  7.4 175.9 %exchange_and_multiply.1 = (f32[512,896]{1,0:T(8,128)}, bf16[128,14336]{1,0:T(8,128)(2,1)}) custom-call(bf16[2,256,896]{2,1,0:T(8,128)(2,1)} %bitcast.1, bf16[128,4096]{1,0:T(8,128)(2,1)} %tok_in.1, bf16[128,14336]{1,0:T(8,128)(2,1)} %cot_in.1), custom_call_target="tpu_custom_call" | custom-call | flops 30064771072 | bytes 16777216 | tf_op jit(solution)/shard_map/exchange_and_multiply/pallas_call | solution.py:362
  183.3 0.0 copy-start
  183.3 3.0 %copy.13 = f32[512,896]{1,0:T(8,128)} copy(f32[512,896]{1,0:T(8,128)} %get-tuple-element.21) | data formatting | bytes 3670016
  186.3 0.0 copy-done
  186.3 1.8 copy.14
Async XLA Ops:
  183.3 3.0 %copy-start = (bf16[128,14336]{1,0:T(8,128)(2,1)S(1)}, bf16[128,14336]{1,0:T(8,128)(2,1)}, u32[]{:S(2)}) copy-start(bf16[128,14336]{1,0:T(8,128)(2,1)} %get-tuple-element.22) | copy-start | bytes 11010052

commit v3 on v2

--- a/solution.py
+++ b/solution.py
@@ -33,56 +33,69 @@
 SCHEDULE = (
     ("cotangent_far", 2),
     ("exchange", 2),
+    ("exchange", 0),
+    ("weight_own",),
+    ("weight_across",),
     ("cotangent_near",),
-    ("exchange", 0),
-    ("weight_across",),
+    ("pair", 0),
     ("exchange", 1),
-    ("weight_own",),
+    ("cotangent_far", 1),
     ("cotangent_far", 3),
+    ("gathered_own", 0),
     ("weight_relay", 0),
-    ("pair", 0),
-    ("cotangent_far", 1),
+    ("pair", 2),
+    ("weight_second",),
+    ("relay", 0),
+    ("exchange", 3),
     ("cotangent_far", 0),
-    ("exchange", 3),
-    ("pair", 2),
-    ("gathered_own", 2),
-    ("relay", 0),
-    ("weight_second",),
+    ("weight_relay", 1),
     ("relay", 2),
     ("pair", 1),
-    ("weight_relay", 1),
+    ("pair", 3),
+    ("gathered_own", 2),
+    ("cross", 2),
+    ("gathered_near", 0),
+    ("gathered_own", 1),
+    ("weight_wait",),
     ("share", 0),
+    ("gathered_own", 3),
+    ("forward_own",),
+    ("gathered_far", 0),
     ("cotangent_wait",),
-    ("weight_wait",),
-    ("gathered_own", 0),
-    ("gathered", 0),
     ("gradient", 0, 1),
+    ("gradient", 0, 0),
+    ("forward_near", 0),
+    ("gathered_near", 2),
+    ("relay", 1),
     ("share", 2),
-    ("gradient", 0, 0),
-    ("pair", 3),
-    ("gathered_own", 1),
-    ("gathered", 2),
+    ("forward_far", 0),
+    ("forward_near", 2),
+    ("gathered_near", 1),
+    ("relay", 3),
+    ("cross", 1),
+    ("forward_near", 1),
+    ("gathered_near", 3),
+    ("forward_last", 1),
+    ("gathered_far", 2),
+    ("forward_last", 3),
+    ("share", 1),
+    ("share", 3),
+    ("gradient", 2, 1),
+    ("gathered_far", 1),
     ("gradient", 2, 0),
-    ("forward", 0),
-    ("gathered_own", 3),
-    ("relay", 1),
-    ("forward_own",),
-    ("relay", 3),
-    ("forward", 2),
-    ("share", 1),
-    ("gradient", 2, 1),
-    ("gathered", 1),
-    ("forward", 1),
-    ("share", 3),
-    ("gathered", 3),
-    ("forward_last", 3),
+    ("forward_far", 1),
+    ("gathered_far", 3),
+    ("forward_far", 2),
+    ("gradient", 1, 0),
+    ("closing_send", 1),
     ("forward_last", 2),
-    ("forward_last", 1),
     ("gradient", 1, 1),
-    ("gradient", 1, 0),
-    ("closing", 1),
-    ("closing", 0),
+    ("closing_send", 0),
+    ("closing_own", 1),
+    ("closing_own", 0),
 )
+
+CROSSING = tuple(q for name, *(q, *_) in [(*step, 0) for step in SCHEDULE] if name == "cross")
 
 
 def adam_update(master_weight, first_moment, second_moment, prior_grad):
@@ -100,7 +113,7 @@
     tok, wts, cot, acc, up, gsend, relay_in, zin, xsend, xin, gown,
     own_t, own_c, own_w, own_u, own_g,
     cot_s, cot_r, out_s, out_r, tx_s, tx_r, ty_s, ty_r, tr_s, tr_r, ts_s, ts_r,
-    wx_s, wx_r, wz_s, wz_r, wr_s, wr_r, g0_s, g0_r, gz_s, gz_r, gx_s, gx_r,
+    tc_s, tc_r, wx_s, wx_r, wz_s, wz_r, wr_s, wr_r, g0_s, g0_r, gz_s, gz_r, gx_s, gx_r,
 ):
     rep, grp = lax.axis_index("rep"), lax.axis_index("grp")
     xl, z = rep // 4, rep % 4
@@ -186,27 +199,53 @@
         send(block, block, ty_s.at[q, 1], ty_r.at[q, 1], in_group(3, 0, 0))
         to_sibling(q, pair_rows(c, 0), 0)
 
+    def from_opposite(q, i):
+        if q in CROSSING:
+            return pl.ds(pl.multiple_of(row(c, 2, xh) + i * (ROWS // 2), ROWS // 2), ROWS // 2)
+        return block_rows(c, 2, i)
+
     def relay(q):
         for i, back, to in ((0, 3, 1), (1, 1, 3)):
             arrived(tok.at[q, pair_rows(c, back)], ty_r.at[q, i])
-            onward = tok.at[q, block_rows(c, back, i)]
+            if q in CROSSING:
+                first = pl.multiple_of(row(c, back, xh) + i * (ROWS // 2), ROWS // 2)
+                onward = tok.at[q, pl.ds(first, ROWS // 2)]
+            else:
+                onward = tok.at[q, block_rows(c, back, i)]
             send(onward, onward, tr_s.at[q, i], tr_r.at[q, i], in_group(to, 0, 0))
         to_sibling(q, pair_rows(c, 3), 1)
         to_sibling(q, pair_rows(c, 1), 2)
 
+    def cross(q):
+        for i in range(2):
+            arrived(tok.at[q, from_opposite(q, i)], tr_r.at[q, i])
+        block = tok.at[q, block_rows(c, 2, xh)]
+        send(block, block, tc_s.at[q], tc_r.at[q], in_group(0, 1, 0))
+        to_sibling(q, block_rows(c, 2, xh), 3)
+
     def share(q):
+        if q in CROSSING:
+            arrived(tok.at[q, block_rows(c, 2, 1 - xh)], tc_r.at[q])
+            to_sibling(q, block_rows(c, 2, 1 - xh), 4)
+            return
         for i in range(2):
-            arrived(tok.at[q, block_rows(c, 2, i)], tr_r.at[q, i])
+            arrived(tok.at[q, from_opposite(q, i)], tr_r.at[q, i])
             to_sibling(q, block_rows(c, 2, i), 3 + i)
 
     def gathered_own(q):
         arrived(tok.at[q, pair_rows(1 - c, 0)], ts_r.at[q, 0])
 
-    def gathered(q):
+    def gathered_near(q):
         for i, dy in ((1, 3), (2, 1)):
             arrived(tok.at[q, pair_rows(1 - c, dy)], ts_r.at[q, i])
-        for i in range(2):
-            arrived(tok.at[q, block_rows(1 - c, 2, i)], ts_r.at[q, 3 + i])
+
+    def gathered_far(q):
+        if q in CROSSING:
+            arrived(tok.at[q, block_rows(1 - c, 2, xh)], ts_r.at[q, 3])
+            arrived(tok.at[q, block_rows(1 - c, 2, 1 - xh)], ts_r.at[q, 4])
+        else:
+            arrived(tok.at[q, block_rows(1 - c, 2, 0)], ts_r.at[q, 3])
+            arrived(tok.at[q, block_rows(1 - c, 2, 1)], ts_r.at[q, 4])
 
     def cotangent_to(i):
         to = in_group(*PARTNERS[i])
@@ -261,52 +300,58 @@
             tok[q, :, pl.ds(first, HALF)], cot[...], (((0,), (0,)), ((), ())), preferred_element_type=F32
         )
 
-    def gradient_piece(q, h, add):
-        def tile(m, carry):
-            first = pl.multiple_of(h * PIECE + m * HALF, HALF)
+    def rows_for(i):
+        return pl.ds(pl.multiple_of((xl if i else 1 - xl) * HALF, HALF), HALF)
+
+    def gradient(q, h):
+        to = in_rep(0, 3 if h else 1)
+        for i in range(2):
+            here = rows_for(i)
+            first = pl.multiple_of(h * PIECE + (xl if i else 1 - xl) * HALF, HALF)
             value = gradient_tile(q, first)
-            if add is not None:
-                value = value + add[pl.ds(pl.multiple_of(m * HALF, HALF), HALF), :].astype(F32)
+            if q == h + 1:
+                arrived(relay_in.at[h, here], g0_r.at[h, i])
+                value = value + relay_in[h, here, :].astype(F32)
             gsend[q, pl.ds(first, HALF), :] = value.astype(BF16)
-            return carry
-
-        lax.fori_loop(0, 2, tile, 0)
-
-    def gradient(q, h):
-        relayed = q == h + 1
-        if relayed:
-            arrived(relay_in.at[h], g0_r.at[h])
-        gradient_piece(q, h, relay_in.at[h] if relayed else None)
-        src, to = gsend.at[q, pl.ds(h * PIECE, PIECE)], in_rep(0, 3 if h else 1)
-        if q:
-            send(src, zin.at[q - 1, h], gz_s.at[q - 1, h], gz_r.at[q - 1, h], to)
-        else:
-            send(src, relay_in.at[h], g0_s.at[h], g0_r.at[h], to)
-
-    def closing_tile(h, a):
-        here = pl.ds(pl.multiple_of(a * HALF, HALF), HALF)
-        value = gradient_tile(3, pl.multiple_of(h * PIECE + a * HALF, HALF))
+            src = gsend.at[q, pl.ds(first, HALF)]
+            if q:
+                dst = zin.at[q - 1, h, here]
+                send(src, dst, gz_s.at[q - 1, h, i], gz_r.at[q - 1, h, i], to)
+            else:
+                send(src, relay_in.at[h, here], g0_s.at[h, i], g0_r.at[h, i], to)
+
+    def closing_tile(h, i):
+        here = rows_for(i)
+        for j in range(2):
+            arrived(zin.at[h, j, here], gz_r.at[h, j, i])
+        value = gradient_tile(3, pl.multiple_of(h * PIECE + (xl if i else 1 - xl) * HALF, HALF))
         return value + zin[h, 0, here, :].astype(F32) + zin[h, 1, here, :].astype(F32)
 
-    def closing(h):
-        for i in range(2):
-            arrived(zin.at[h, i], gz_r.at[h, i])
+    def closing_send(h):
         here = pl.ds(h * HALF, HALF)
-        xsend[here, :] = closing_tile(h, 1 - xl).astype(BF16)
+        xsend[here, :] = closing_tile(h, 0).astype(BF16)
         send(xsend.at[here], xin.at[here], gx_s.at[h], gx_r.at[h], in_rep(1, 0))
-        gown[here, :] = closing_tile(h, xl)
+
+    def closing_own(h):
+        gown[pl.ds(h * HALF, HALF), :] = closing_tile(h, 1)
 
     def forward_block(q, rows):
         return jnp.dot(tok[q, rows, :], wts[q].reshape(QUARTER, COLS), preferred_element_type=F32)
 
-    def forward(q):
+    def forward_rows(q, dys):
         def block(i, carry):
-            rows = pair_rows(i // 3, 1 + i % 3)
+            rows = pair_rows(i // len(dys), dys[0] + 2 * (i % len(dys)))
             value = forward_block(q, rows)
             acc[rows, :] = value + acc[rows, :] if q else value
             return carry
 
-        lax.fori_loop(0, 6, block, 0)
+        lax.fori_loop(0, 2 * len(dys), block, 0)
+
+    def forward_near(q):
+        forward_rows(q, (1, 3))
+
+    def forward_far(q):
+        forward_rows(q, (2,))
 
     def home(dy, dc):
         core = (c + dc) % 2
@@ -333,9 +378,9 @@
     steps = {
         f.__name__: f
         for f in (
-            exchange, pair, relay, share, gathered_own, gathered, cotangent_near, cotangent_far, cotangent_wait,
+            exchange, pair, relay, cross, share, gathered_own, gathered_near, gathered_far, cotangent_near, cotangent_far, cotangent_wait,
             weight_own, weight_across, weight_second, weight_relay, weight_wait,
-            gradient, forward, forward_own, forward_last, closing,
+            gradient, forward_near, forward_far, forward_own, forward_last, closing_send, closing_own,
         )
     }
     for name, *which in SCHEDULE:
@@ -386,11 +431,12 @@
             dma((4, 2)), dma((4, 2)),
             dma((4, 2)), dma((4, 2)),
             dma((4, 5)), dma((4, 5)),
+            dma((4,)), dma((4,)),
             dma((1,)), dma((1,)),
             dma((2, 2)), dma((2, 2)),
             dma((2, 2)), dma((2, 2)),
-            dma((2,)), dma((2,)),
             dma((2, 2)), dma((2, 2)),
+            dma((2, 2, 2)), dma((2, 2, 2)),
             dma((2,)), dma((2,)),
         ],
         compiler_params=pltpu.CompilerParams(

time: 188 us -> 178 us (0.947)
  Pallas kernels: 176 us -> 165 us
    pallas_call x1, Pallas kernels: 176 us -> 165 us  [exchange_and_multiply(): pl.pallas_call(kernel, out_shape=(jax.ShapeDtypeStruct((PIECE, COLS), F32...]
where the time goes in v3:
time: 178 us
  Pallas kernels  165 us (93%)
  other arithmetic  6.77 us (4%)
  local copies, waits for them, and re-layouts  4.84 us (3%)
    pallas_call x1, Pallas kernels, exchange_and_multiply(): pl.pallas_call(kernel, out_shape=(jax.ShapeDtypeStruct((PIECE, COLS), F32...  165 us
    convert_element_type x1, other arithmetic, body(): weight_half = new_master.astype(BF16)  6.77 us
    unnamed x4, local copies, waits for them, and re-layouts  4.84 us

profile of v3, /device:TPU:1, one launch (start us, length us, event | category | flops | bytes accessed | tf_op | source)
XLA Modules:
  0.0 177.7 jit_solution(9716871972933209031)
XLA Ops:
  0.6 6.8 %fusion.1 = (bf16[512,896]{1,0:T(8,128)(2,1)}, f32[512,896]{1,0:T(8,128)}, f32[512,896]{1,0:T(8,128)}, f32[512,896]{1,0:T(8,128)}) fusion(f32[512,896]{1,0:T(8,128)} %param.6, f32[512,896]{1,0:T(8,128)} %param.9, f32[512,896]{1,0:T(8,128)} %param.7, f32[512,896]{1,0:T(8,128)} %param.8), kind=kLoop, calls=%fused_computation.4 | loop fusion | flops 7340032 | bytes 13762560 | tf_op jit(solution)/shard_map/convert_element_type | solution.py:456
  7.4 165.5 %exchange_and_multiply.1 = (f32[512,896]{1,0:T(8,128)}, bf16[128,14336]{1,0:T(8,128)(2,1)}) custom-call(bf16[2,256,896]{2,1,0:T(8,128)(2,1)} %bitcast.1, bf16[128,4096]{1,0:T(8,128)(2,1)} %tok_in.1, bf16[128,14336]{1,0:T(8,128)(2,1)} %cot_in.1), custom_call_target="tpu_custom_call" | custom-call | flops 30064771072 | bytes 16777216 | tf_op jit(solution)/shard_map/exchange_and_multiply/pallas_call | solution.py:407
  172.9 0.0 copy-start
  172.9 3.0 %copy.13 = f32[512,896]{1,0:T(8,128)} copy(f32[512,896]{1,0:T(8,128)} %get-tuple-element.21) | data formatting | bytes 3670016
  175.9 0.0 copy-done
  175.9 1.8 %copy.14 = bf16[128,14336]{1,0:T(8,128)(2,1)} copy(bf16[128,14336]{1,0:T(8,128)(2,1)S(1)} %copy-done) | data formatting | bytes 7340032
Async XLA Ops:
  172.9 3.0 %copy-start = (bf16[128,14336]{1,0:T(8,128)(2,1)S(1)}, bf16[128,14336]{1,0:T(8,128)(2,1)}, u32[]{:S(2)}) copy-start(bf16[128,14336]{1,0:T(8,128)(2,1)} %get-tuple-element.22) | copy-start | bytes 11010052

commit v4 on v3

--- a/solution.py
+++ b/solution.py
@@ -12,6 +12,8 @@
 beta_two = 0.95
 epsilon = 1e-08
 decay_weight = 0.1
+bias_one = 1.0 - beta_one**STEP
+bias_two = 1.0 - beta_two**STEP
 
 MESH = pl.DeviceIdType.MESH
 BF16, F32 = jnp.bfloat16, jnp.float32
@@ -24,6 +26,7 @@
 PAIR = 2 * ROWS
 GROUP = 16 * ROWS
 QUARTER = 1024
+STRIP = 32
 
 PARTNERS = sorted(
     [(dy, dx, dc) for dy in range(4) for dx in range(2) for dc in range(2) if (dy, dx, dc) != (0, 0, 0)],
@@ -34,6 +37,7 @@
     ("cotangent_far", 2),
     ("exchange", 2),
     ("exchange", 0),
+    ("adam",),
     ("weight_own",),
     ("weight_across",),
     ("cotangent_near",),
@@ -98,20 +102,11 @@
 CROSSING = tuple(q for name, *(q, *_) in [(*step, 0) for step in SCHEDULE] if name == "cross")
 
 
-def adam_update(master_weight, first_moment, second_moment, prior_grad):
-    first_new = beta_one * first_moment + (1.0 - beta_one) * prior_grad
-    second_new = beta_two * second_moment + (1.0 - beta_two) * prior_grad * prior_grad
-    bias_one = 1.0 - beta_one**STEP
-    bias_two = 1.0 - beta_two**STEP
-    step_size = first_new / bias_one / (jnp.sqrt(second_new / bias_two) + epsilon)
-    new_master = master_weight - learning_rate * (step_size + decay_weight * master_weight)
-    return (new_master, first_new, second_new)
-
-
 def kernel(
-    w_in, tok_in, cot_in, grad_out, up_out,
-    tok, wts, cot, acc, up, gsend, relay_in, zin, xsend, xin, gown,
-    own_t, own_c, own_w, own_u, own_g,
+    master_in, first_in, second_in, prior_in, tok_in, cot_in,
+    master, first_moment, second_moment, grad_out, up_out,
+    tok, wts, cot, acc, up, gsend, relay_in, zin, xin,
+    own_t, own_c, own_a, own_u,
     cot_s, cot_r, out_s, out_r, tx_s, tx_r, ty_s, ty_r, tr_s, tr_r, ts_s, ts_r,
     tc_s, tc_r, wx_s, wx_r, wz_s, wz_r, wr_s, wr_r, g0_s, g0_r, gz_s, gz_r, gx_s, gx_r,
 ):
@@ -131,6 +126,7 @@
         copy = pltpu.make_async_remote_copy(src, dst, ss, rs, device_id=to, device_id_type=MESH)
         copy.start()
         sends.append(copy)
+        return copy
 
     def arrived(ref, rs):
         pltpu.make_async_remote_copy(
@@ -148,12 +144,6 @@
 
     def columns(device):
         return pl.ds(pl.multiple_of(device * COLS, 128), COLS)
-
-    barrier = pltpu.get_barrier_semaphore()
-    peers = [in_group(*t) for t in PARTNERS] + [in_rep(0, 1), in_rep(0, 3), in_rep(1, 0)]
-    for peer in peers:
-        pl.semaphore_signal(barrier, inc=1, device_id=peer, device_id_type=MESH)
-    pl.semaphore_wait(barrier, len(peers))
 
     own = block_rows(c, 0, xh)
     own_tokens = {}
@@ -171,15 +161,22 @@
                 own_tokens[q, h, a] = copy
     own_cot = pltpu.make_async_copy(cot_in.at[:, columns(grp)], cot.at[own], own_c.at[0])
     own_cot.start()
-    own_weight = pltpu.make_async_copy(w_in, wts.at[3, :, xl], own_w.at[0])
-    own_weight.start()
+    prior = acc.at[pl.ds(0, PIECE)]
+    own_adam = [
+        pltpu.make_async_copy(src, dst, own_a.at[i])
+        for i, (src, dst) in enumerate(
+            ((master_in, master), (first_in, first_moment), (second_in, second_moment), (prior_in, prior))
+        )
+    ]
+    for copy in own_adam:
+        copy.start()
     own_up = pltpu.make_async_copy(up.at[own], up_out.at[:, columns(grp)], own_u.at[0])
-    own_grad = [
-        pltpu.make_async_copy(
-            gown.at[pl.ds(h * HALF, HALF)], grad_out.at[pl.ds(h * HALF, HALF)], own_g.at[h]
-        )
-        for h in range(2)
-    ]
+
+    barrier = pltpu.get_barrier_semaphore()
+    peers = [in_group(*t) for t in PARTNERS] + [in_rep(0, 1), in_rep(0, 3), in_rep(1, 0)]
+    for peer in peers:
+        pl.semaphore_signal(barrier, inc=1, device_id=peer, device_id_type=MESH)
+    pl.semaphore_wait(barrier, len(peers))
 
     def to_sibling(q, rows, i):
         block = tok.at[q, rows]
@@ -266,8 +263,29 @@
         for i, (dy, dx, dc) in enumerate(PARTNERS):
             arrived(cot.at[block_rows((c - dc) % 2, -dy, (xh - dx) % 2)], cot_r.at[i])
 
+    def adam():
+        for copy in own_adam:
+            copy.wait()
+        for h in range(2):
+
+            def some(i, carry):
+                here = pl.ds(pl.multiple_of(h * HALF + i * STRIP, STRIP), STRIP)
+                gradient = prior[here, :]
+                weight = master[here, :]
+                first_new = beta_one * first_moment[here, :] + (1.0 - beta_one) * gradient
+                second_new = beta_two * second_moment[here, :] + (1.0 - beta_two) * gradient * gradient
+                step_size = first_new / bias_one / (jnp.sqrt(second_new / bias_two) + epsilon)
+                weight = weight - learning_rate * (step_size + decay_weight * weight)
+                first_moment[here, :] = first_new
+                second_moment[here, :] = second_new
+                master[here, :] = weight
+                wts[3, h, xl, pl.ds(pl.multiple_of(i * STRIP, STRIP), STRIP), :] = weight.astype(BF16)
+                return carry
+
+            lax.fori_loop(0, HALF // STRIP, some, 0)
+
     def spread(order, a):
-        src = wts.at[3, :, a] if order else w_in
+        src = wts.at[3, :, a]
         send(src, wts.at[pl.ds(1, 2), 1, a], wz_s.at[order, 0], wz_r.at[order, 0], in_rep(0, 1))
         send(src, wts.at[pl.ds(1, 2), 0, a], wz_s.at[order, 1], wz_r.at[order, 1], in_rep(0, 3))
 
@@ -275,7 +293,8 @@
         spread(0, xl)
 
     def weight_across():
-        send(w_in, wts.at[3, :, xl], wx_s.at[0], wx_r.at[0], in_rep(1, 0))
+        block = wts.at[3, :, xl]
+        send(block, block, wx_s.at[0], wx_r.at[0], in_rep(1, 0))
 
     def weight_second():
         arrived(wts.at[3, :, 1 - xl], wx_r.at[0])
@@ -293,7 +312,6 @@
             a = 1 - xl if order else xl
             for h in range(2):
                 arrived(wts.at[0, h, a], wr_r.at[order, h])
-        own_weight.wait()
 
     def gradient_tile(q, first):
         return lax.dot_general(
@@ -302,6 +320,8 @@
 
     def rows_for(i):
         return pl.ds(pl.multiple_of((xl if i else 1 - xl) * HALF, HALF), HALF)
+
+    first_sends = {}
 
     def gradient(q, h):
         to = in_rep(0, 3 if h else 1)
@@ -312,13 +332,16 @@
             if q == h + 1:
                 arrived(relay_in.at[h, here], g0_r.at[h, i])
                 value = value + relay_in[h, here, :].astype(F32)
-            gsend[q, pl.ds(first, HALF), :] = value.astype(BF16)
-            src = gsend.at[q, pl.ds(first, HALF)]
+            if q == 1:
+                sends[:] = [copy for copy in sends if copy is not first_sends[h, i]]
+                first_sends[h, i].wait_send()
+            gsend[q // 2, pl.ds(first, HALF), :] = value.astype(BF16)
+            src = gsend.at[q // 2, pl.ds(first, HALF)]
             if q:
                 dst = zin.at[q - 1, h, here]
                 send(src, dst, gz_s.at[q - 1, h, i], gz_r.at[q - 1, h, i], to)
             else:
-                send(src, relay_in.at[h, here], g0_s.at[h, i], g0_r.at[h, i], to)
+                first_sends[h, i] = send(src, relay_in.at[h, here], g0_s.at[h, i], g0_r.at[h, i], to)
 
     def closing_tile(h, i):
         here = rows_for(i)
@@ -328,21 +351,25 @@
         return value + zin[h, 0, here, :].astype(F32) + zin[h, 1, here, :].astype(F32)
 
     def closing_send(h):
-        here = pl.ds(h * HALF, HALF)
-        xsend[here, :] = closing_tile(h, 0).astype(BF16)
-        send(xsend.at[here], xin.at[here], gx_s.at[h], gx_r.at[h], in_rep(1, 0))
+        out = relay_in.at[h, pl.ds(0, HALF)]
+        out[...] = closing_tile(h, 0).astype(BF16)
+        send(out, xin.at[pl.ds(h * HALF, HALF)], gx_s.at[h], gx_r.at[h], in_rep(1, 0))
 
     def closing_own(h):
-        gown[pl.ds(h * HALF, HALF), :] = closing_tile(h, 1)
+        grad_out[pl.ds(h * HALF, HALF), :] = closing_tile(h, 1)
 
     def forward_block(q, rows):
         return jnp.dot(tok[q, rows, :], wts[q].reshape(QUARTER, COLS), preferred_element_type=F32)
 
+    def acc_rows(core, dy):
+        return pl.ds(pl.multiple_of((core * 3 + dy - 1) * PAIR, PAIR), PAIR)
+
     def forward_rows(q, dys):
         def block(i, carry):
-            rows = pair_rows(i // len(dys), dys[0] + 2 * (i % len(dys)))
-            value = forward_block(q, rows)
-            acc[rows, :] = value + acc[rows, :] if q else value
+            core, dy = i // len(dys), dys[0] + 2 * (i % len(dys))
+            value = forward_block(q, pair_rows(core, dy))
+            kept = acc_rows(core, dy)
+            acc[kept, :] = value + acc[kept, :] if q else value
             return carry
 
         lax.fori_loop(0, 2 * len(dys), block, 0)
@@ -371,15 +398,16 @@
 
     def forward_last(dy):
         for dc in range(2):
-            rows = pair_rows((c + dc) % 2, dy)
-            up[rows, :] = (forward_block(3, rows) + acc[rows, :]).astype(BF16)
+            core = (c + dc) % 2
+            rows = pair_rows(core, dy)
+            up[rows, :] = (forward_block(3, rows) + acc[acc_rows(core, dy), :]).astype(BF16)
             home(dy, dc)
 
     steps = {
         f.__name__: f
         for f in (
             exchange, pair, relay, cross, share, gathered_own, gathered_near, gathered_far, cotangent_near, cotangent_far, cotangent_wait,
-            weight_own, weight_across, weight_second, weight_relay, weight_wait,
+            adam, weight_own, weight_across, weight_second, weight_relay, weight_wait,
             gradient, forward_near, forward_far, forward_own, forward_last, closing_send, closing_own,
         )
     }
@@ -389,42 +417,35 @@
     for h in range(2):
         here = pl.ds(h * HALF, HALF)
         arrived(xin.at[here], gx_r.at[h])
-        gown[here, :] = gown[here, :] + xin[here, :].astype(F32)
-        own_grad[h].start()
+        grad_out[here, :] = grad_out[here, :] + xin[here, :].astype(F32)
     for i, (dy, dx, dc) in enumerate(PARTNERS):
         source = ((y - dy) % 4) * 4 + ((xh - dx) % 2) * 2 + (c - dc) % 2
         arrived(up_out.at[:, columns(source)], out_r.at[i])
     own_up.wait()
-    for copy in own_grad:
-        copy.wait()
     for copy in sends:
         copy.wait_send()
 
 
-def exchange_and_multiply(weight_half, tokens, cotangent):
+def update_exchange_and_multiply(master, first_moment, second_moment, prior_grad, tokens, cotangent):
     dma = pltpu.SemaphoreType.DMA
     n = len(PARTNERS)
+    shard = pltpu.VMEM((PIECE, COLS), F32)
     return pl.pallas_call(
         kernel,
-        out_shape=(
-            jax.ShapeDtypeStruct((PIECE, COLS), F32),
-            jax.ShapeDtypeStruct((ROWS, 16 * COLS), BF16),
-        ),
-        in_specs=[pl.BlockSpec(memory_space=pl.ANY)] * 3,
-        out_specs=(pl.BlockSpec(memory_space=pl.ANY),) * 2,
+        out_shape=(shard, shard, shard, shard, pltpu.VMEM((ROWS, 16 * COLS), BF16)),
+        in_specs=[pl.BlockSpec(memory_space=pl.ANY)] * 6,
+        out_specs=(pl.BlockSpec(memory_space=pltpu.VMEM),) * 5,
         scratch_shapes=[
             pltpu.VMEM((4, GROUP, QUARTER), BF16),
             pltpu.VMEM((4, 2, 2, HALF, COLS), BF16),
             pltpu.VMEM((GROUP, COLS), BF16),
-            pltpu.VMEM((GROUP, COLS), F32),
+            pltpu.VMEM((6 * PAIR, COLS), F32),
             pltpu.VMEM((GROUP, COLS), BF16),
-            pltpu.VMEM((3, QUARTER, COLS), BF16),
+            pltpu.VMEM((2, QUARTER, COLS), BF16),
             pltpu.VMEM((2, PIECE, COLS), BF16),
             pltpu.VMEM((2, 2, PIECE, COLS), BF16),
             pltpu.VMEM((PIECE, COLS), BF16),
-            pltpu.VMEM((PIECE, COLS), BF16),
-            pltpu.VMEM((PIECE, COLS), F32),
-            dma((4, 4)), dma((1,)), dma((1,)), dma((1,)), dma((2,)),
+            dma((4, 4)), dma((1,)), dma((4,)), dma((1,)),
             dma((n,)), dma((n,)),
             dma((n,)), dma((n,)),
             dma((4,)), dma((4,)),
@@ -440,27 +461,18 @@
             dma((2,)), dma((2,)),
         ],
         compiler_params=pltpu.CompilerParams(
-            collective_id=0, has_side_effects=True, vmem_limit_bytes=62 * 2**20
+            collective_id=0, has_side_effects=True, vmem_limit_bytes=53 * 2**20
         ),
         cost_estimate=pl.CostEstimate(
             flops=4 * GROUP * WIDE * COLS, bytes_accessed=16 * 2**20, transcendentals=0
         ),
-        name="exchange_and_multiply",
-    )(weight_half.reshape(2, HALF, COLS), tokens, cotangent)
-
-
-def body(master_weight, first_moment, second_moment, prior_grad, tokens, cotangent):
-    new_master, first_new, second_new = adam_update(
-        master_weight, first_moment, second_moment, prior_grad
-    )
-    weight_half = new_master.astype(BF16)
-    grad_sum, up_proj = exchange_and_multiply(weight_half, tokens, cotangent)
-    return (new_master, first_new, second_new, grad_sum, up_proj)
+        name="update_exchange_and_multiply",
+    )(master, first_moment, second_moment, prior_grad, tokens, cotangent)
 
 
 def solution(mesh):
     return jax.shard_map(
-        body,
+        update_exchange_and_multiply,
         mesh=mesh,
         in_specs=(
             P("rep", "grp"),

time: 178 us -> 173 us (0.972)
  other arithmetic: 6.77 us -> 0 us
  local copies, waits for them, and re-layouts: 4.84 us -> 6.75 us
    convert_element_type x1 -> x0, other arithmetic: 6.77 us -> none  [body(): weight_half = new_master.astype(BF16)]
    unnamed x4 -> x5, local copies, waits for them, and re-layouts: 4.84 us -> 6.75 us
where the time goes in v4:
time: 173 us; the launch traced here: 172 us
  Pallas kernels  165 us (95%)
  local copies, waits for them, and re-layouts  6.75 us (4%)
    pallas_call x1, Pallas kernels, update_exchange_and_multiply(): pl.pallas_call(kernel, out_shape=(shard, shard, shard, shard, pltpu.VMEM(...  165 us
    unnamed x5, local copies, waits for them, and re-layouts  6.75 us

profile of v4, /device:TPU:1, one launch (start us, length us, event | category | flops | bytes accessed | tf_op | source)
XLA Modules:
  0.0 172.0 jit_solution(4193160705444636080)
XLA Ops:
  0.6 164.6 %update_exchange_and_multiply.1 = (f32[512,896]{1,0:T(8,128)S(1)}, f32[512,896]{1,0:T(8,128)S(1)}, f32[512,896]{1,0:T(8,128)S(1)}, f32[512,896]{1,0:T(8,128)S(1)}, bf16[128,14336]{1,0:T(8,128)(2,1)S(1)}) custom-call(f32[512,896]{1,0:T(8,128)} %master_in.1, f32[512,896]{1,0:T(8,128)} %first_in.1, f32[512,896]{1,0:T(8,128)} %second_in.1, f32[512,896]{1,0:T(8,128)} %prior_in.1, ...), custom_call_target="tpu_custom_call" | custom-call | flops 30064771072 | bytes 16777216 | tf_op jit(solution)/shard_map/update_exchange_and_multiply/pallas_call | solution.py:433
  165.3 1.2 copy.16
  166.5 1.2 copy.17
  167.7 1.2 copy.18
  168.9 1.2 copy.19
  170.2 1.8 %copy.20 = bf16[128,14336]{1,0:T(8,128)(2,1)} copy(bf16[128,14336]{1,0:T(8,128)(2,1)S(1)} %get-tuple-element.9) | data formatting | bytes 7340032

commit v5 on v4

--- a/solution.py
+++ b/solution.py
@@ -35,66 +35,66 @@
 
 SCHEDULE = (
     ("cotangent_far", 2),
-    ("exchange", 2),
+    ("cotangent_near",),
     ("exchange", 0),
+    ("exchange", 1),
     ("adam",),
     ("weight_own",),
     ("weight_across",),
-    ("cotangent_near",),
+    ("weight_relay", 0),
+    ("exchange", 2),
+    ("exchange", 3),
     ("pair", 0),
-    ("exchange", 1),
-    ("cotangent_far", 1),
-    ("cotangent_far", 3),
+    ("cotangent_far", 0),
+    ("pair", 1),
     ("gathered_own", 0),
-    ("weight_relay", 0),
-    ("pair", 2),
     ("weight_second",),
     ("relay", 0),
-    ("exchange", 3),
-    ("cotangent_far", 0),
+    ("cotangent_far", 3),
+    ("relay", 1),
+    ("cotangent_far", 1),
+    ("pair", 3),
+    ("gathered_own", 3),
+    ("pair", 2),
+    ("cross", 1),
+    ("gathered_near", 0),
     ("weight_relay", 1),
-    ("relay", 2),
-    ("pair", 1),
-    ("pair", 3),
+    ("share", 0),
     ("gathered_own", 2),
-    ("cross", 2),
-    ("gathered_near", 0),
+    ("gathered_far", 0),
+    ("weight_wait",),
     ("gathered_own", 1),
-    ("weight_wait",),
-    ("share", 0),
-    ("gathered_own", 3),
     ("forward_own",),
-    ("gathered_far", 0),
+    ("forward_near", 0),
     ("cotangent_wait",),
     ("gradient", 0, 1),
+    ("relay", 3),
+    ("gathered_near", 1),
     ("gradient", 0, 0),
-    ("forward_near", 0),
-    ("gathered_near", 2),
-    ("relay", 1),
-    ("share", 2),
-    ("forward_far", 0),
-    ("forward_near", 2),
-    ("gathered_near", 1),
-    ("relay", 3),
-    ("cross", 1),
     ("forward_near", 1),
     ("gathered_near", 3),
+    ("relay", 2),
+    ("cross", 3),
+    ("share", 1),
+    ("gathered_near", 2),
+    ("forward_near", 2),
+    ("gathered_far", 1),
     ("forward_last", 1),
+    ("gradient", 1, 1),
+    ("forward_last", 3),
+    ("gradient", 1, 0),
+    ("forward_far", 0),
+    ("share", 3),
+    ("share", 2),
     ("gathered_far", 2),
-    ("forward_last", 3),
-    ("share", 1),
-    ("share", 3),
-    ("gradient", 2, 1),
-    ("gathered_far", 1),
-    ("gradient", 2, 0),
+    ("forward_far", 2),
     ("forward_far", 1),
     ("gathered_far", 3),
-    ("forward_far", 2),
-    ("gradient", 1, 0),
+    ("closing_send", 0),
+    ("forward_last", 2),
+    ("gradient", 2, 0),
+    ("gradient", 2, 1),
     ("closing_send", 1),
-    ("forward_last", 2),
-    ("gradient", 1, 1),
-    ("closing_send", 0),
     ("closing_own", 1),
     ("closing_own", 0),
 )

time: 173 us -> 172 us (level)
  no operation moved by 1% of the time
where the time goes in v5:
time: 172 us
  Pallas kernels  165 us (96%)
  local copies, waits for them, and re-layouts  6.75 us (4%)
    pallas_call x1, Pallas kernels, update_exchange_and_multiply(): pl.pallas_call(kernel, out_shape=(shard, shard, shard, shard, pltpu.VMEM(...  165 us
    unnamed x5, local copies, waits for them, and re-layouts  6.75 us

profile of v5, /device:TPU:1, one launch (start us, length us, event | category | flops | bytes accessed | tf_op | source)
XLA Modules:
  0.0 172.1 jit_solution(10633362616211669513)
XLA Ops:
  0.6 164.7 %update_exchange_and_multiply.1 = (f32[512,896]{1,0:T(8,128)S(1)}, f32[512,896]{1,0:T(8,128)S(1)}, f32[512,896]{1,0:T(8,128)S(1)}, f32[512,896]{1,0:T(8,128)S(1)}, bf16[128,14336]{1,0:T(8,128)(2,1)S(1)}) custom-call(f32[512,896]{1,0:T(8,128)} %master_in.1, f32[512,896]{1,0:T(8,128)} %first_in.1, f32[512,896]{1,0:T(8,128)} %second_in.1, f32[512,896]{1,0:T(8,128)} %prior_in.1, ...), custom_call_target="tpu_custom_call" | custom-call | flops 30064771072 | bytes 16777216 | tf_op jit(solution)/shard_map/update_exchange_and_multiply/pallas_call | solution.py:433
  165.4 1.2 copy.16
  166.6 1.2 copy.17
  167.8 1.2 copy.18
  169.0 1.2 copy.19
  170.3 1.8 %copy.20 = bf16[128,14336]{1,0:T(8,128)(2,1)} copy(bf16[128,14336]{1,0:T(8,128)(2,1)S(1)} %get-tuple-element.9) | data formatting | bytes 7340032
